TPU v7x, 128 devices: a whole 4x4x4 slice. The times are simulated.
128 devices in a mesh: dev: 128 (over y, z, x, core).
Axes of the slice: x: 4, y: 4, z: 4, core: 2. Of those that a mesh axis runs over, the one named last changes fastest.
Arguments:
- density_rows: bfloat16 [98304, 3840], P('dev')
- center_x: float32 [98304], replicated, may hold values from -0.25 to 1.25
- center_y: float32 [98304], replicated, may hold values from 0 to 1
- center_z: float32 [98304], replicated, may hold values from 0 to 1
- exponent: float32 [98304], replicated, may hold values from 0.5 to 150
- brick_blocks: int32 [128, 8], replicated, may hold values from 0 to 767, as said below
Outputs:
- potential: float32 [128, 4096], P('dev')
- ham_rows: float32 [98304, 3840], P('dev')
Inputs may be any that keep to these rules, and one draw needn't show every extreme that they name: `brick_blocks`: brick b belongs to device d = b. Its 8 entries are distinct blocks; 4 of them are owned by one of the devices d - 1, d, d + 1 (cyclically) and 2 by each of the other two, where block I is owned by device I // 6. Which of the three owns 4 changes from brick to brick. Blocks 0 and 767 touch brick 0.
All inputs are finite; a program needn't handle non-finite values.
Results may differ from a plain program's by a relative error of at most 0.00041.
Values may be sent and summed in bfloat16 or wider, within the bound.
No kernel may reach another device: no remote copies, remote signals or barrier semaphores. Data moves between devices by JAX's collectives and lax.ppermute only.
A program may use at most 128 MiB of HBM per device.

v0:
```python
import math

import jax
import jax.numpy as jnp
from jax import lax
from jax.experimental import pallas as pl
from jax.experimental.pallas import tpu as pltpu
from jax.sharding import PartitionSpec as P

FB = 128
KB = 8
BLK_DEV = 6
SIDE = 16
LAYER = SIDE * SIDE
CELLS = SIDE * LAYER
WIDE = KB * FB
CHUNK = 1024
SUB = 256
PAIR = 2 * FB
TILE = 8
TILES = 5
COLS = 5 * BLK_DEV

omega = 2.0 / 3.0
four_pi = 4.0 * math.pi
slater = (3.0 / math.pi) ** (1.0 / 3.0)

VMEM = pl.BlockSpec(memory_space=pltpu.VMEM)
SMEM = pl.BlockSpec(memory_space=pltpu.SMEM)
HBM = pl.BlockSpec(memory_space=pltpu.HBM)
LIMIT = 536 * 2**20 // 10


def aligned(index, unit):
    return pl.ds(pl.multiple_of(index * unit, unit), unit)


def wrap(value, count):
    return lax.rem(value + 2 * count, count)


def list_blocks(devices, sides, bricks_ref, lists_ref, count_ref):
    own = lax.axis_index("dev")
    for side in sides:
        brick = wrap(own + side - 1, devices)
        ids = [bricks_ref[k, brick] for k in range(KB)]
        owners = [i // BLK_DEV for i in ids]
        held = [(owner == own).astype(jnp.int32) for owner in owners]
        first, second = jnp.int32(0), sum(held)
        count_ref[side] = second
        for i, owner, h in zip(ids, owners, held):
            at = side * KB + jnp.where(h == 1, first, second)
            row = i - owner * BLK_DEV
            lists_ref[0, at] = i
            lists_ref[1, at] = row
            lists_ref[2, at] = wrap(owner - own + 2, devices) * BLK_DEV + row
            lists_ref[3, at] = owner
            first, second = first + h, second + 1 - h


def first_tile(devices):
    own = lax.axis_index("dev")
    return wrap((own - 2) * BLK_DEV, devices * BLK_DEV) // TILE


def fetch_tables(devices, table_refs, tables_ref, sem):
    base = first_tile(devices)
    for t, table_ref in enumerate(table_refs):
        for k in range(TILES):
            tile = lax.rem(base + k, devices * BLK_DEV // TILE)
            pltpu.make_async_copy(
                table_ref.at[aligned(tile, TILE), :], tables_ref.at[t, pl.ds(k * TILE, TILE), :], sem
            ).start()


def factors(devices, side, lists_ref, tables_ref, x_ref, y_ref, z_ref):
    own = lax.axis_index("dev")
    brick = wrap(own + side - 1, devices)
    base = first_tile(devices) * TILE
    points = (lax.broadcasted_iota(jnp.int32, (SIDE, FB), 0).astype(jnp.float32) + 0.5) / SIDE
    for k in range(KB):
        block, owner = lists_ref[0, side * KB + k], lists_ref[3, side * KB + k]
        offset = (wrap(brick - owner + 1, devices) - 1).astype(jnp.float32)
        row = pl.ds(wrap(block - base, devices * BLK_DEV), 1)
        decay = -tables_ref[3, row, :]
        lanes = pl.ds(k * FB, FB)
        along_x = (offset + points) - tables_ref[0, row, :]
        x_ref[:, lanes] = jnp.exp(decay * along_x * along_x)
        for t, out_ref in ((1, y_ref), (2, z_ref)):
            away = points - tables_ref[t, row, :] + 0.5
            away = away - jnp.floor(away) - 0.5
            out_ref[:, lanes] = jnp.exp(decay * away * away)


def orbital_chunk(part, step, x_ref, y_ref, z_ref, orb_ref):
    layers = CHUNK // LAYER
    for k in range(KB):
        lanes = slice(k * FB, (k + 1) * FB)
        x = x_ref[aligned(step, 8), lanes]
        y, z = y_ref[:, lanes], z_ref[:, lanes]
        for i in range(layers):
            xy = x[part * layers + i : part * layers + i + 1] * y
            for j in range(SIDE):
                at = (i * SIDE + j) * SIDE
                orb_ref[at : at + SIDE, lanes] = (xy[j : j + 1] * z).astype(jnp.bfloat16)


def density_of(
    devices, sides, bricks_ref, table_refs, rows_ref,
    lists_ref, count_ref, tables_ref, x_ref, y_ref, z_ref, orb_a, orb_b, dens_ref, res_ref, table_sem, dens_sems,
):
    first, stride = sides
    fetch_tables(devices, table_refs, tables_ref, table_sem)
    slots = dens_ref.shape[0]
    list_blocks(devices, [first + stride * slot for slot in range(slots)], bricks_ref, lists_ref, count_ref)

    def fetch_brick(slot, carry):
        side = first + stride * slot

        def fetch(half, inner):
            for a in range(2):
                row = lists_ref[1, side * KB + half * 2 + a]
                for c in range(KB):
                    pltpu.make_async_copy(
                        rows_ref.at[aligned(row, FB), aligned(lists_ref[2, side * KB + c], FB)],
                        dens_ref.at[slot, aligned(half * 2 + a, FB), pl.ds(c * FB, FB)],
                        dens_sems.at[slot, half],
                    ).start()
            return inner

        return lax.fori_loop(0, count_ref[side] // 2, fetch, carry)

    lax.fori_loop(0, slots, fetch_brick, 0)
    pltpu.make_async_copy(tables_ref, tables_ref, table_sem).wait()

    def one_brick(slot, carry):
        side = first + stride * slot
        factors(devices, side, lists_ref, tables_ref, x_ref, y_ref, z_ref)

        def await_half(half, inner):
            pltpu.make_async_copy(
                rows_ref.at[pl.ds(0, PAIR), pl.ds(0, WIDE)],
                dens_ref.at[slot, aligned(half, PAIR), :],
                dens_sems.at[slot, half],
            ).wait()
            return inner

        lax.fori_loop(0, count_ref[side] // 2, await_half, 0)

        def steps(rows):
            def step(t, inner):
                for part, orb_ref in ((0, orb_a), (1, orb_b)):
                    orbital_chunk(part, t, x_ref, y_ref, z_ref, orb_ref)
                    for s in range(0, CHUNK, SUB):
                        applied = lax.dot_general(
                            orb_ref[s : s + SUB, :], dens_ref[slot, :rows, :], (((1,), (1,)), ((), ())),
                            preferred_element_type=jnp.float32,
                        )
                        product = applied * orb_ref[s : s + SUB, :rows].astype(jnp.float32)
                        total = product[:, :FB]
                        for k in range(FB, rows, FB):
                            total = total + product[:, k : k + FB]
                        at = pl.ds(pl.multiple_of(t * 2 * CHUNK + part * CHUNK + s, SUB), SUB)
                        res_ref[slot, :, at] = jnp.sum(total.T, axis=0, keepdims=True)
                return inner

            lax.fori_loop(0, CELLS // (2 * CHUNK), step, 0)

        pl.when(count_ref[side] == 2)(lambda: steps(PAIR))
        pl.when(count_ref[side] != 2)(lambda: steps(2 * PAIR))
        return carry

    lax.fori_loop(0, slots, one_brick, 0)


def folded(row):
    total = row[:, :FB]
    for k in range(1, CELLS // FB):
        total = total + row[:, k * FB : (k + 1) * FB]
    return total


def odd_device():
    return lax.rem(lax.axis_index("dev"), 2)


def beside_kernel(devices, bricks_ref, cx_ref, cy_ref, cz_ref, ex_ref, rows_ref, mate_ref, far_ref, charge_ref, *scratch):
    density_of(devices, (0, 2), bricks_ref, (cx_ref, cy_ref, cz_ref, ex_ref), rows_ref, *scratch)
    res_ref = scratch[9]
    odd = odd_device()
    mate_ref[...] = res_ref[1 - odd]
    far_ref[...] = res_ref[odd]
    charge_ref[...] = folded(res_ref[0] + res_ref[1])


def own_kernel(
    devices, bricks_ref, cx_ref, cy_ref, cz_ref, ex_ref, rows_ref, mate_ref, charge_ref,
    pack_ref, total_ref, zero_out_ref, *scratch
):
    zero_ref, zero_sems = scratch[-2:]
    zero_ref[...] = jnp.zeros_like(zero_ref)
    zero_copies = [
        pltpu.make_async_copy(zero_ref, zero_out_ref.at[pl.ds(r * FB, FB), :], zero_sems.at[r]) for r in range(BLK_DEV)
    ]
    for copy in zero_copies:
        copy.start()
    density_of(devices, (1, 0), bricks_ref, (cx_ref, cy_ref, cz_ref, ex_ref), rows_ref, *scratch[:-2])
    res_ref = scratch[9]
    pack_ref[:, :CELLS] = mate_ref[...]
    pack_ref[:, CELLS:] = res_ref[0]
    total_ref[...] = charge_ref[...] + folded(res_ref[0])
    for copy in zero_copies:
        copy.wait()


def add_kernel(pack_ref, mate_pack_ref, far_ref, mate_far_ref, total_ref, own_ref, mate_ref, charges_ref):
    own = pack_ref[:, CELLS:] + mate_pack_ref[:, :CELLS] + far_ref[...]
    mate = pack_ref[:, :CELLS] + mate_pack_ref[:, CELLS:] + mate_far_ref[...]
    own_ref[:, :CELLS] = own
    own_ref[:, CELLS:] = jnp.where(odd_device() == 1, mate[:, CELLS - LAYER :], mate[:, :LAYER])
    mate_ref[...] = mate
    charges_ref[...] = jnp.broadcast_to(total_ref[...][None], charges_ref.shape)


def potential_of(density, before, after, average):
    lane = lax.broadcasted_iota(jnp.int32, density.shape, 1)
    along_z = lane & (SIDE - 1)
    along_y = (lane // SIDE) & (SIDE - 1)
    scale = omega * four_pi / 6.0
    source = density - average
    one = scale * source
    padded = jnp.concatenate([scale * (before - average), one, scale * (after - average)], axis=1)
    beside = padded[:, :CELLS] + padded[:, 2 * LAYER :]

    def moved(steps):
        return pltpu.roll(one, steps % CELLS, 1)

    beside += jnp.where(along_y > 0, moved(SIDE), moved(SIDE - LAYER))
    beside += jnp.where(along_y < SIDE - 1, moved(-SIDE), moved(LAYER - SIDE))
    beside += jnp.where(along_z > 0, moved(1), moved(1 - SIDE))
    beside += jnp.where(along_z < SIDE - 1, moved(-1), moved(SIDE - 1))
    two = one + omega * ((four_pi * source + beside) / 6.0 - one)
    root = jnp.exp(jnp.log(jnp.abs(density)) * (1.0 / 3.0))
    return two - slater * jnp.where(density < 0.0, -root, root)


def ham_kernel(
    devices, bricks_ref, cx_ref, cy_ref, cz_ref, ex_ref,
    own_ref, mate_ref, far_ref, mate_far_ref, charges_ref, zeroed_ref,
    pot_ref, ham_ref,
    lists_ref, count_ref, tables_ref, x_ref, y_ref, z_ref, orb_a, orb_b, v_ref, acc_ref, sum_ref,
    table_sem, ham_sems, clear_sem,
):
    fetch_tables(devices, (cx_ref, cy_ref, cz_ref, ex_ref), tables_ref, table_sem)
    clearing = pltpu.make_async_copy(ham_ref, sum_ref, clear_sem)
    clearing.start()
    list_blocks(devices, range(3), bricks_ref, lists_ref, count_ref)

    def wide(row):
        return jnp.broadcast_to(row, (8, row.shape[1]))

    odd = odd_device() == 1
    mate, far = mate_ref[...], far_ref[:, :CELLS]
    far_edge, mate_edge = far_ref[:, CELLS:], jnp.where(odd, mate_far_ref[:, CELLS - LAYER : CELLS], mate_far_ref[:, :LAYER])
    mid = wide(own_ref[:, :CELLS])
    left, right = wide(jnp.where(odd, mate, far)), wide(jnp.where(odd, far, mate))
    before, after = wide(jnp.where(odd, mate_edge, far_edge)), wide(jnp.where(odd, far_edge, mate_edge))
    average = jnp.sum(jnp.sum(charges_ref[...], axis=0)) / (devices * CELLS)
    scale = 64.0 / CELLS
    v_ref[0] = scale * potential_of(left, before, mid[:, :LAYER], average)
    own_potential = potential_of(mid, left[:, CELLS - LAYER :], right[:, :LAYER], average)
    v_ref[1] = scale * own_potential
    v_ref[2] = scale * potential_of(right, mid[:, CELLS - LAYER :], after, average)
    pot_ref[...] = own_potential[:1]
    pltpu.make_async_copy(tables_ref, tables_ref, table_sem).wait()

    def await_rows(side, rows_half):
        pltpu.make_async_copy(
            sum_ref.at[pl.ds(0, PAIR), pl.ds(0, WIDE)], ham_ref.at[pl.ds(0, PAIR), pl.ds(0, WIDE)],
            ham_sems.at[side, rows_half],
        ).wait()

    def await_brick(side):
        lax.fori_loop(0, count_ref[side] // 2, lambda half, inner: (await_rows(side, half), inner)[1], 0)

    def one_brick(side, carry):
        factors(devices, side, lists_ref, tables_ref, x_ref, y_ref, z_ref)

        def steps(rows):
            def step(t, inner):
                for part, orb_ref in ((0, orb_a), (1, orb_b)):
                    orbital_chunk(part, t, x_ref, y_ref, z_ref, orb_ref)
                    at = pl.ds(pl.multiple_of(t * 2 * CHUNK + part * CHUNK, CHUNK), CHUNK)
                    v = v_ref[side, pl.ds(0, 1), at]
                    mine = orb_ref[:, :rows].T
                    weighted = (mine.astype(jnp.float32) * v).astype(jnp.bfloat16)
                    for r in range(0, rows, PAIR):
                        acc_ref[r : r + PAIR, r:] += jnp.dot(
                            weighted[r : r + PAIR], orb_ref[:, r:], preferred_element_type=jnp.float32
                        )
                return inner

            acc_ref[:rows, :] = jnp.zeros((rows, WIDE), jnp.float32)
            lax.fori_loop(0, CELLS // (2 * CHUNK), step, 0)
            if rows > PAIR:
                acc_ref[PAIR:rows, :PAIR] = acc_ref[:PAIR, PAIR:rows].T
            pl.when(side == 0)(clearing.wait)
            pl.when(side > 0)(lambda: await_brick(jnp.maximum(side - 1, 0)))
            for a in range(rows // FB):
                row = lists_ref[1, side * KB + a]
                for c in range(KB):
                    block = (aligned(row, FB), aligned(lists_ref[2, side * KB + c], FB))
                    sum_ref[block] += acc_ref[a * FB : (a + 1) * FB, c * FB : (c + 1) * FB]
                    pltpu.make_async_copy(sum_ref.at[block], ham_ref.at[block], ham_sems.at[side, a // 2]).start()

        pl.when(count_ref[side] == 2)(lambda: steps(PAIR))
        pl.when(count_ref[side] != 2)(lambda: steps(2 * PAIR))
        return carry

    lax.fori_loop(0, 3, one_brick, 0)
    await_brick(2)


def f32(*shape):
    return jax.ShapeDtypeStruct(shape, jnp.float32)


def solution(mesh):
    devices = mesh.shape["dev"]

    def with_mate(value):
        return lax.ppermute(value, "dev", [(i, i ^ 1) for i in range(devices)])

    def with_far(value):
        return lax.ppermute(value, "dev", [(i, (i + (i % 2) * 2 - 1) % devices) for i in range(devices)])

    shared_scratch = [
        pltpu.SMEM((4, 3 * KB), jnp.int32),
        pltpu.SMEM((3,), jnp.int32),
        pltpu.VMEM((4, TILES * TILE, FB), jnp.float32),
        pltpu.VMEM((SIDE, WIDE), jnp.float32),
        pltpu.VMEM((SIDE, WIDE), jnp.float32),
        pltpu.VMEM((SIDE, WIDE), jnp.float32),
        pltpu.VMEM((CHUNK, WIDE), jnp.bfloat16),
        pltpu.VMEM((CHUNK, WIDE), jnp.bfloat16),
    ]

    def local(density_rows, center_x, center_y, center_z, exponent, brick_blocks):
        tables = [t.reshape(-1, FB) for t in (center_x, center_y, center_z, exponent)]
        bricks = brick_blocks.T
        params = pltpu.CompilerParams(vmem_limit_bytes=LIMIT)

        def density_scratch(slots):
            return shared_scratch + [
                pltpu.VMEM((slots, 2 * PAIR, WIDE), jnp.bfloat16),
                pltpu.VMEM((slots, 1, CELLS), jnp.float32),
                pltpu.SemaphoreType.DMA(()),
                pltpu.SemaphoreType.DMA((slots, 2)),
            ]

        for_mate, for_far, charge = pl.pallas_call(
            lambda *refs: beside_kernel(devices, *refs),
            out_shape=[f32(1, CELLS), f32(1, CELLS), f32(1, FB)],
            in_specs=[SMEM] + [HBM] * 5,
            out_specs=[VMEM] * 3,
            scratch_shapes=density_scratch(2),
            compiler_params=params,
        )(bricks, *tables, density_rows)
        far_part = with_far(for_far)
        pack, total, zeroed = pl.pallas_call(
            lambda *refs: own_kernel(devices, *refs),
            out_shape=[f32(1, 2 * CELLS), f32(1, FB), f32(BLK_DEV * FB, COLS * FB)],
            in_specs=[SMEM] + [HBM] * 5 + [VMEM] * 2,
            out_specs=[VMEM, VMEM, HBM],
            scratch_shapes=density_scratch(1)
            + [pltpu.VMEM((FB, COLS * FB), jnp.float32), pltpu.SemaphoreType.DMA((BLK_DEV,))],
            compiler_params=params,
            cost_estimate=pl.CostEstimate(flops=8 * 10**9, bytes_accessed=2 * 10**7, transcendentals=0),
        )(bricks, *tables, density_rows, for_mate, charge)
        mate_pack = with_mate(pack)
        mate_far_part = with_mate(far_part)
        own, mate, charges = pl.pallas_call(
            add_kernel,
            out_shape=[f32(1, CELLS + LAYER), f32(1, CELLS), f32(devices, 1, FB)],
            in_specs=[VMEM] * 5,
            out_specs=[VMEM] * 3,
            compiler_params=pltpu.CompilerParams(vmem_limit_bytes=8 * 2**20),
        )(pack, mate_pack, far_part, mate_far_part, total)
        far = with_far(own)
        charges = lax.all_to_all(charges, "dev", 0, 0, tiled=True)
        mate_far = with_mate(far)
        return pl.pallas_call(
            lambda *refs: ham_kernel(devices, *refs),
            out_shape=[f32(1, CELLS), f32(BLK_DEV * FB, COLS * FB)],
            in_specs=[SMEM] + [HBM] * 4 + [VMEM] * 5 + [HBM],
            out_specs=[VMEM, HBM],
            scratch_shapes=shared_scratch
            + [
                pltpu.VMEM((3, 8, CELLS), jnp.float32),
                pltpu.VMEM((2 * PAIR, WIDE), jnp.float32),
                pltpu.VMEM((BLK_DEV * FB, COLS * FB), jnp.float32),
                pltpu.SemaphoreType.DMA(()),
                pltpu.SemaphoreType.DMA((3, 2)),
                pltpu.SemaphoreType.DMA(()),
            ],
            input_output_aliases={10: 1},
            compiler_params=params,
        )(bricks, *tables, own, mate, far, mate_far, charges, zeroed)

    return jax.shard_map(
        local,
        mesh=mesh,
        in_specs=(P("dev", None), P(), P(), P(), P(), P()),
        out_specs=(P("dev", None), P("dev", None)),
        check_vma=False,
    )
```

profile of v0, /device:TPU:1, one launch (start us, length us, event | category | flops | bytes accessed | tf_op | source)
XLA Modules:
  0.0 64.0 jit_solution(17926419248822738101)
XLA Ops:
  0.6 0.0 copy-start
  0.6 0.7 %copy-done = s32[128,8]{0,1:T(8,128)S(1)} copy-done((s32[128,8]{0,1:T(8,128)S(1)}, s32[128,8]{0,1:T(8,128)}, u32[]{:S(2)}) %copy-start) | copy-done | bytes 4120
  1.3 10.5 %shard_map.77 = (f32[1,4096]{1,0:T(1,128)S(1)}, f32[1,4096]{1,0:T(1,128)S(1)}, f32[1,128]{1,0:T(1,128)S(1)}) custom-call(s32[8,128]{1,0:T(8,128)S(1)} %bitcast.5, f32[768,128]{1,0:T(8,128)} %bitcast.8, f32[768,128]{1,0:T(8,128)} %bitcast.11, f32[768,128]{1,0:T(8,128)} %bitcast.14, f32[768,128]{1,0:T(8,128)} %bitcast.17, bf16[768,3840]{1,0:T(8,128)(2,1)} %refs_5_.3), custom_call_target="tpu_custom_call" | custom-call | tf_op jit(solution)/shard_map/pallas_call | solution.py:361
  11.9 0.6 collective-permute-start.1
  12.5 0.0 copy-start.1
  12.5 6.1 %shard_map.78 = (f32[1,8192]{1,0:T(1,128)S(1)}, f32[1,128]{1,0:T(1,128)S(1)}, f32[768,3840]{1,0:T(8,128)}) custom-call(s32[8,128]{1,0:T(8,128)S(1)} %bitcast.6, f32[768,128]{1,0:T(8,128)} %bitcast.9, f32[768,128]{1,0:T(8,128)} %bitcast.12, f32[768,128]{1,0:T(8,128)} %bitcast.15, f32[768,128]{1,0:T(8,128)} %bitcast.18, bf16[768,3840]{1,0:T(8,128)(2,1)} %refs_5_.3, ...), custom_call_target="tpu_custom_call" | custom-call | flops 8000000000 | bytes 20000000 | tf_op jit(solution)/shard_map/pallas_call | solution.py:370
  18.7 9.2 %collective-permute-start = (f32[1,8192]{1,0:T(1,128)S(1)}, f32[1,8192]{1,0:T(1,128)S(1)}, u32[]{:S(2)}, u32[]{:S(2)}) collective-permute-start(f32[1,8192]{1,0:T(1,128)S(1)} %get-tuple-element.13.pack_ref), channel_id=1, source_target_pairs={{0,1},{1,0},{2,3},{3,2},{4,5},{5,4},{6,7},{7,6},{8,9},{9,8},{10,11... | collective-permute-start | bytes 98312 | tf_op jit(solution)/shard_map/ppermute | solution.py:332
  27.8 0.0 collective-permute-done.1.far_ref
  27.8 0.1 collective-permute-start.2
  27.9 1.1 %collective-permute-done.2.mate_far_ref = f32[1,4096]{1,0:T(1,128)S(1)} collective-permute-done((f32[1,4096]{1,0:T(1,128)S(1)}, f32[1,4096]{1,0:T(1,128)S(1)}, u32[]{:S(2)}, u32[]{:S(2)}) %collective-permute-start.2) | collective-permute-done | bytes 16416 | tf_op jit(solution)/shard_map/ppermute | solution.py:332
  29.0 0.0 collective-permute-done.mate_pack_ref
  29.0 0.7 %shard_map.79 = (f32[1,4352]{1,0:T(1,128)S(1)}, f32[1,4096]{1,0:T(1,128)S(1)}, f32[128,1,128]{2,1,0:T(1,128)}) custom-call(f32[1,8192]{1,0:T(1,128)S(1)} %get-tuple-element.13.pack_ref, f32[1,8192]{1,0:T(1,128)S(1)} %collective-permute-done.mate_pack_ref, f32[1,4096]{1,0:T(1,128)S(1)} %collective-permute-done.1.far_ref, ...), custom_call_target="tpu_custom_call" | custom-call | tf_op jit(solution)/shard_map/pallas_call | solution.py:382
  29.7 6.1 %all-to-all-start = ((f32[128,1,128]{2,1,0:T(1,128)}), f32[128,1,128]{2,1,0:T(1,128)S(1)}, u32[]{:S(2)}, u32[]{:S(2)}) async-start(f32[128,1,128]{2,1,0:T(1,128)} %get-tuple-element.18), calls=%async_computation | async-start | bytes 131072 | tf_op jit(solution)/shard_map/all_to_all | solution.py:390
  35.8 1.7 %collective-permute-start.3 = (f32[1,4352]{1,0:T(1,128)S(1)}, f32[1,4352]{1,0:T(1,128)S(1)}, u32[]{:S(2)}, u32[]{:S(2)}) collective-permute-start(f32[1,4352]{1,0:T(1,128)S(1)} %get-tuple-element.16.refs_5_), channel_id=1, source_target_pairs={{0,127},{1,2},{2,1},{3,4},{4,3},{5,6},{6,5},{7,8},{8,7},{9,10},{10... | collective-permute-start | bytes 52232 | tf_op jit(solution)/shard_map/ppermute | solution.py:335
  37.5 1.8 %collective-permute-done.3.refs_7_ = f32[1,4352]{1,0:T(1,128)S(1)} collective-permute-done((f32[1,4352]{1,0:T(1,128)S(1)}, f32[1,4352]{1,0:T(1,128)S(1)}, u32[]{:S(2)}, u32[]{:S(2)}) %collective-permute-start.3) | collective-permute-done | bytes 17440 | tf_op jit(solution)/shard_map/ppermute | solution.py:335
  39.3 6.4 %collective-permute-start.4 = (f32[1,4352]{1,0:T(1,128)S(1)}, f32[1,4352]{1,0:T(1,128)S(1)}, u32[]{:S(2)}, u32[]{:S(2)}) collective-permute-start(f32[1,4352]{1,0:T(1,128)S(1)} %collective-permute-done.3.refs_7_), channel_id=1, source_target_pairs={{0,1},{1,0},{2,3},{3,2},{4,5},{5,4},{6,7},{7,6},{8,9},{9,8},{10,11... | collective-permute-start | bytes 52232 | tf_op jit(solution)/shard_map/ppermute | solution.py:332
  45.7 0.8 %collective-permute-done.4.refs_8_ = f32[1,4352]{1,0:T(1,128)S(1)} collective-permute-done((f32[1,4352]{1,0:T(1,128)S(1)}, f32[1,4352]{1,0:T(1,128)S(1)}, u32[]{:S(2)}, u32[]{:S(2)}) %collective-permute-start.4) | collective-permute-done | bytes 17440 | tf_op jit(solution)/shard_map/ppermute | solution.py:332
  46.6 0.0 all-to-all-done.refs_9_
  46.6 0.0 copy-done.1
  46.6 17.3 %shard_map.80 = (f32[1,4096]{1,0:T(1,128)}, f32[768,3840]{1,0:T(8,128)}) custom-call(s32[8,128]{1,0:T(8,128)S(1)} %bitcast.7, f32[768,128]{1,0:T(8,128)} %bitcast.10, f32[768,128]{1,0:T(8,128)} %bitcast.13, f32[768,128]{1,0:T(8,128)} %bitcast.16, f32[768,128]{1,0:T(8,128)} %bitcast.19, ...), custom_call_target="tpu_custom_call", output_to_operand_aliasing={{1}: (10, {})} | custom-call | tf_op jit(solution)/shard_map/pallas_call | solution.py:392
Async XLA Ops:
  0.6 0.7 %copy-start = (s32[128,8]{0,1:T(8,128)S(1)}, s32[128,8]{0,1:T(8,128)}, u32[]{:S(2)}) copy-start(s32[128,8]{0,1:T(8,128)} %param.11) | copy-start | bytes 12292
  11.9 15.9 %collective-permute-start.1 = (f32[1,4096]{1,0:T(1,128)S(1)}, f32[1,4096]{1,0:T(1,128)S(1)}, u32[]{:S(2)}, u32[]{:S(2)}) collective-permute-start(f32[1,4096]{1,0:T(1,128)S(1)} %get-tuple-element.14), channel_id=1, source_target_pairs={{0,127},{1,2},{2,1},{3,4},{4,3},{5,6},{6,5},{7,8},{8,7},{9,10},{10... | collective-permute-start | bytes 49160 | tf_op jit(solution)/shard_map/ppermute | solution.py:335
  12.5 34.1 %copy-start.1 = (s32[128,8]{0,1:T(8,128)S(1)}, s32[128,8]{0,1:T(8,128)}, u32[]{:S(2)}) copy-start(s32[128,8]{0,1:T(8,128)} %param.11) | copy-start | bytes 12292
  18.7 10.3 %collective-permute-start = (f32[1,8192]{1,0:T(1,128)S(1)}, f32[1,8192]{1,0:T(1,128)S(1)}, u32[]{:S(2)}, u32[]{:S(2)}) collective-permute-start(f32[1,8192]{1,0:T(1,128)S(1)} %get-tuple-element.13.pack_ref), channel_id=1, source_target_pairs={{0,1},{1,0},{2,3},{3,2},{4,5},{5,4},{6,7},{7,6},{8,9},{9,8},{10,11... | collective-permute-start | bytes 98312 | tf_op jit(solution)/shard_map/ppermute | solution.py:332
  27.8 1.2 %collective-permute-start.2 = (f32[1,4096]{1,0:T(1,128)S(1)}, f32[1,4096]{1,0:T(1,128)S(1)}, u32[]{:S(2)}, u32[]{:S(2)}) collective-permute-start(f32[1,4096]{1,0:T(1,128)S(1)} %collective-permute-done.1.far_ref), channel_id=1, source_target_pairs={{0,1},{1,0},{2,3},{3,2},{4,5},{5,4},{6,7},{7,6},{8,9},{9,8},{10,11... | collective-permute-start | bytes 49160 | tf_op jit(solution)/shard_map/ppermute | solution.py:332
  29.7 16.9 %all-to-all-start = ((f32[128,1,128]{2,1,0:T(1,128)}), f32[128,1,128]{2,1,0:T(1,128)S(1)}, u32[]{:S(2)}, u32[]{:S(2)}) async-start(f32[128,1,128]{2,1,0:T(1,128)} %get-tuple-element.18), calls=%async_computation | async-start | bytes 131072 | tf_op jit(solution)/shard_map/all_to_all | solution.py:390
  35.8 3.5 %collective-permute-start.3 = (f32[1,4352]{1,0:T(1,128)S(1)}, f32[1,4352]{1,0:T(1,128)S(1)}, u32[]{:S(2)}, u32[]{:S(2)}) collective-permute-start(f32[1,4352]{1,0:T(1,128)S(1)} %get-tuple-element.16.refs_5_), channel_id=1, source_target_pairs={{0,127},{1,2},{2,1},{3,4},{4,3},{5,6},{6,5},{7,8},{8,7},{9,10},{10... | collective-permute-start | bytes 52232 | tf_op jit(solution)/shard_map/ppermute | solution.py:335
  39.3 7.3 %collective-permute-start.4 = (f32[1,4352]{1,0:T(1,128)S(1)}, f32[1,4352]{1,0:T(1,128)S(1)}, u32[]{:S(2)}, u32[]{:S(2)}) collective-permute-start(f32[1,4352]{1,0:T(1,128)S(1)} %collective-permute-done.3.refs_7_), channel_id=1, source_target_pairs={{0,1},{1,0},{2,3},{3,2},{4,5},{5,4},{6,7},{7,6},{8,9},{9,8},{10,11... | collective-permute-start | bytes 52232 | tf_op jit(solution)/shard_map/ppermute | solution.py:332
where the time goes:
time: 64.7 us; the launch traced here: 64 us
  Pallas kernels  34.6 us (53%)
  starting transfers between devices  24.1 us (37%)
  waiting for transfers between devices  3.77 us (6%)
  between operations  0.83 us (1%)
  local copies, waits for them, and re-layouts  0.69 us (1%)
    pallas_call x1, Pallas kernels, local(): pl.pallas_call(lambda *refs: ham_kernel(devices, *refs), out_shape=[f32(1...  17.3 us
    ppermute x3, starting transfers between devices, with_mate(): return lax.ppermute(value, 'dev', [(i, i ^ 1) for i in range(devices)])  15.7 us
    pallas_call x1, Pallas kernels, local(): pl.pallas_call(lambda *refs: beside_kernel(devices, *refs), out_shape=[f3...  10.5 us
    pallas_call x1, Pallas kernels, local(): pl.pallas_call(lambda *refs: own_kernel(devices, *refs), out_shape=[f32(1...  6.13 us
    all_to_all x1, starting transfers between devices, local(): charges = lax.all_to_all(charges, 'dev', 0, 0, tiled=True)  6.11 us
    ppermute x2, starting transfers between devices, with_far(): lax.ppermute(value, 'dev', [(i, (i + i % 2 * 2 - 1) % devices) for i in r...  2.35 us
    ppermute x3, waiting for transfers between devices, with_mate(): return lax.ppermute(value, 'dev', [(i, i ^ 1) for i in range(devices)])  1.93 us
    ppermute x2, waiting for transfers between devices, with_far(): lax.ppermute(value, 'dev', [(i, (i + i % 2 * 2 - 1) % devices) for i in r...  1.84 us
  transfers between devices with their start and end apart: 6, of which 3 were waited for; matrix products, arithmetic and copies ran while one was open for 0% of the time, Pallas kernels for 10%

commit v1 on v0

--- a/solution.py
+++ b/solution.py
@@ -32,6 +32,8 @@
 
 
 def aligned(index, unit):
+    if isinstance(index, int):
+        return pl.ds(index * unit, unit)
     return pl.ds(pl.multiple_of(index * unit, unit), unit)
 
 
@@ -148,7 +150,7 @@
         lax.fori_loop(0, count_ref[side] // 2, await_half, 0)
 
         def steps(rows):
-            def step(t, inner):
+            def step(t):
                 for part, orb_ref in ((0, orb_a), (1, orb_b)):
                     orbital_chunk(part, t, x_ref, y_ref, z_ref, orb_ref)
                     for s in range(0, CHUNK, SUB):
@@ -160,11 +162,11 @@
                         total = product[:, :FB]
                         for k in range(FB, rows, FB):
                             total = total + product[:, k : k + FB]
-                        at = pl.ds(pl.multiple_of(t * 2 * CHUNK + part * CHUNK + s, SUB), SUB)
+                        at = pl.ds(t * 2 * CHUNK + part * CHUNK + s, SUB)
                         res_ref[slot, :, at] = jnp.sum(total.T, axis=0, keepdims=True)
-                return inner
-
-            lax.fori_loop(0, CELLS // (2 * CHUNK), step, 0)
+
+            for t in range(CELLS // (2 * CHUNK)):
+                step(t)
 
         pl.when(count_ref[side] == 2)(lambda: steps(PAIR))
         pl.when(count_ref[side] != 2)(lambda: steps(2 * PAIR))
@@ -287,21 +289,21 @@
         factors(devices, side, lists_ref, tables_ref, x_ref, y_ref, z_ref)
 
         def steps(rows):
-            def step(t, inner):
+            def step(t):
                 for part, orb_ref in ((0, orb_a), (1, orb_b)):
                     orbital_chunk(part, t, x_ref, y_ref, z_ref, orb_ref)
-                    at = pl.ds(pl.multiple_of(t * 2 * CHUNK + part * CHUNK, CHUNK), CHUNK)
+                    at = pl.ds(t * 2 * CHUNK + part * CHUNK, CHUNK)
                     v = v_ref[side, pl.ds(0, 1), at]
                     mine = orb_ref[:, :rows].T
                     weighted = (mine.astype(jnp.float32) * v).astype(jnp.bfloat16)
                     for r in range(0, rows, PAIR):
-                        acc_ref[r : r + PAIR, r:] += jnp.dot(
-                            weighted[r : r + PAIR], orb_ref[:, r:], preferred_element_type=jnp.float32
-                        )
-                return inner
-
-            acc_ref[:rows, :] = jnp.zeros((rows, WIDE), jnp.float32)
-            lax.fori_loop(0, CELLS // (2 * CHUNK), step, 0)
+                        product = jnp.dot(weighted[r : r + PAIR], orb_ref[:, r:], preferred_element_type=jnp.float32)
+                        if t + part > 0:
+                            product += acc_ref[r : r + PAIR, r:]
+                        acc_ref[r : r + PAIR, r:] = product
+
+            for t in range(CELLS // (2 * CHUNK)):
+                step(t)
             if rows > PAIR:
                 acc_ref[PAIR:rows, :PAIR] = acc_ref[:PAIR, PAIR:rows].T
             pl.when(side == 0)(clearing.wait)

time: 64.7 us -> 66.5 us (1.028); the launches traced: 64 us -> 66.7 us
  Pallas kernels: 34.6 us -> 37.5 us
    ppermute x3, starting transfers between devices: 15.7 us -> 11.7 us  [with_mate(): return lax.ppermute(value, 'dev', [(i, i ^ 1) for i in range(devices)])]
    ppermute x2, starting transfers between devices: 2.35 us -> 6.28 us  [with_far(): lax.ppermute(value, 'dev', [(i, (i + i % 2 * 2 - 1) % devices) for i in r...]
    pallas_call x1, Pallas kernels: 10.5 us -> 12 us  [local(): pl.pallas_call(lambda *refs: beside_kernel(devices, *refs), out_shape=[f3...]
    pallas_call x1, Pallas kernels: 6.13 us -> 6.88 us  [local(): pl.pallas_call(lambda *refs: own_kernel(devices, *refs), out_shape=[f32(1...]
    pallas_call x1, Pallas kernels: 17.3 us -> 18 us  [local(): pl.pallas_call(lambda *refs: ham_kernel(devices, *refs), out_shape=[f32(1...]
where the time goes in v1:
time: 66.5 us; the launch traced here: 66.7 us
  Pallas kernels  37.5 us (56%)
  starting transfers between devices  23.8 us (36%)
  waiting for transfers between devices  3.77 us (6%)
  between operations  0.85 us (1%)
  local copies, waits for them, and re-layouts  0.69 us (1%)
    pallas_call x1, Pallas kernels, local(): pl.pallas_call(lambda *refs: ham_kernel(devices, *refs), out_shape=[f32(1...  18 us
    pallas_call x1, Pallas kernels, local(): pl.pallas_call(lambda *refs: beside_kernel(devices, *refs), out_shape=[f3...  12 us
    ppermute x3, starting transfers between devices, with_mate(): return lax.ppermute(value, 'dev', [(i, i ^ 1) for i in range(devices)])  11.7 us
    pallas_call x1, Pallas kernels, local(): pl.pallas_call(lambda *refs: own_kernel(devices, *refs), out_shape=[f32(1...  6.88 us
    ppermute x2, starting transfers between devices, with_far(): lax.ppermute(value, 'dev', [(i, (i + i % 2 * 2 - 1) % devices) for i in r...  6.28 us
    all_to_all x1, starting transfers between devices, local(): charges = lax.all_to_all(charges, 'dev', 0, 0, tiled=True)  5.82 us
    ppermute x3, waiting for transfers between devices, with_mate(): return lax.ppermute(value, 'dev', [(i, i ^ 1) for i in range(devices)])  1.93 us
    ppermute x2, waiting for transfers between devices, with_far(): lax.ppermute(value, 'dev', [(i, (i + i % 2 * 2 - 1) % devices) for i in r...  1.84 us
  transfers between devices with their start and end apart: 6, of which 3 were waited for; matrix products, arithmetic and copies ran while one was open for 0% of the time, Pallas kernels for 10%

profile of v1, /device:TPU:1, one launch (start us, length us, event | category | flops | bytes accessed | tf_op | source)
XLA Modules:
  0.0 66.7 jit_solution(14199349432276622044)
XLA Ops:
  0.6 0.0 copy-start
  0.6 0.7 %copy-done = s32[128,8]{0,1:T(8,128)S(1)} copy-done((s32[128,8]{0,1:T(8,128)S(1)}, s32[128,8]{0,1:T(8,128)}, u32[]{:S(2)}) %copy-start) | copy-done | bytes 4120
  1.3 12.0 %shard_map.77 = (f32[1,4096]{1,0:T(1,128)S(1)}, f32[1,4096]{1,0:T(1,128)S(1)}, f32[1,128]{1,0:T(1,128)S(1)}) custom-call(s32[8,128]{1,0:T(8,128)S(1)} %bitcast.5, f32[768,128]{1,0:T(8,128)} %bitcast.8, f32[768,128]{1,0:T(8,128)} %bitcast.11, f32[768,128]{1,0:T(8,128)} %bitcast.14, f32[768,128]{1,0:T(8,128)} %bitcast.17, bf16[768,3840]{1,0:T(8,128)(2,1)} %refs_5_.3), custom_call_target="tpu_custom_call" | custom-call | tf_op jit(solution)/shard_map/pallas_call | solution.py:363
  13.4 4.6 %collective-permute-start.1 = (f32[1,4096]{1,0:T(1,128)S(1)}, f32[1,4096]{1,0:T(1,128)S(1)}, u32[]{:S(2)}, u32[]{:S(2)}) collective-permute-start(f32[1,4096]{1,0:T(1,128)S(1)} %get-tuple-element.14), channel_id=1, source_target_pairs={{0,127},{1,2},{2,1},{3,4},{4,3},{5,6},{6,5},{7,8},{8,7},{9,10},{10... | collective-permute-start | bytes 49160 | tf_op jit(solution)/shard_map/ppermute | solution.py:337
  17.9 0.0 copy-start.1
  17.9 6.9 %shard_map.78 = (f32[1,8192]{1,0:T(1,128)S(1)}, f32[1,128]{1,0:T(1,128)S(1)}, f32[768,3840]{1,0:T(8,128)}) custom-call(s32[8,128]{1,0:T(8,128)S(1)} %bitcast.6, f32[768,128]{1,0:T(8,128)} %bitcast.9, f32[768,128]{1,0:T(8,128)} %bitcast.12, f32[768,128]{1,0:T(8,128)} %bitcast.15, f32[768,128]{1,0:T(8,128)} %bitcast.18, bf16[768,3840]{1,0:T(8,128)(2,1)} %refs_5_.3, ...), custom_call_target="tpu_custom_call" | custom-call | flops 8000000000 | bytes 20000000 | tf_op jit(solution)/shard_map/pallas_call | solution.py:372
  24.8 5.2 %collective-permute-start = (f32[1,8192]{1,0:T(1,128)S(1)}, f32[1,8192]{1,0:T(1,128)S(1)}, u32[]{:S(2)}, u32[]{:S(2)}) collective-permute-start(f32[1,8192]{1,0:T(1,128)S(1)} %get-tuple-element.13.pack_ref), channel_id=1, source_target_pairs={{0,1},{1,0},{2,3},{3,2},{4,5},{5,4},{6,7},{7,6},{8,9},{9,8},{10,11... | collective-permute-start | bytes 98312 | tf_op jit(solution)/shard_map/ppermute | solution.py:334
  30.0 0.0 collective-permute-done.1.far_ref
  30.0 0.1 collective-permute-start.2
  30.1 1.1 %collective-permute-done.2.mate_far_ref = f32[1,4096]{1,0:T(1,128)S(1)} collective-permute-done((f32[1,4096]{1,0:T(1,128)S(1)}, f32[1,4096]{1,0:T(1,128)S(1)}, u32[]{:S(2)}, u32[]{:S(2)}) %collective-permute-start.2) | collective-permute-done | bytes 16416 | tf_op jit(solution)/shard_map/ppermute | solution.py:334
  31.2 0.0 collective-permute-done.mate_pack_ref
  31.2 0.7 shard_map.79
  31.9 5.8 %all-to-all-start = ((f32[128,1,128]{2,1,0:T(1,128)}), f32[128,1,128]{2,1,0:T(1,128)S(1)}, u32[]{:S(2)}, u32[]{:S(2)}) async-start(f32[128,1,128]{2,1,0:T(1,128)} %get-tuple-element.18), calls=%async_computation | async-start | bytes 131072 | tf_op jit(solution)/shard_map/all_to_all | solution.py:392
  37.7 1.7 %collective-permute-start.3 = (f32[1,4352]{1,0:T(1,128)S(1)}, f32[1,4352]{1,0:T(1,128)S(1)}, u32[]{:S(2)}, u32[]{:S(2)}) collective-permute-start(f32[1,4352]{1,0:T(1,128)S(1)} %get-tuple-element.16.refs_5_), channel_id=1, source_target_pairs={{0,127},{1,2},{2,1},{3,4},{4,3},{5,6},{6,5},{7,8},{8,7},{9,10},{10... | collective-permute-start | bytes 52232 | tf_op jit(solution)/shard_map/ppermute | solution.py:337
  39.4 1.8 %collective-permute-done.3.refs_7_ = f32[1,4352]{1,0:T(1,128)S(1)} collective-permute-done((f32[1,4352]{1,0:T(1,128)S(1)}, f32[1,4352]{1,0:T(1,128)S(1)}, u32[]{:S(2)}, u32[]{:S(2)}) %collective-permute-start.3) | collective-permute-done | bytes 17440 | tf_op jit(solution)/shard_map/ppermute | solution.py:337
  41.3 6.4 %collective-permute-start.4 = (f32[1,4352]{1,0:T(1,128)S(1)}, f32[1,4352]{1,0:T(1,128)S(1)}, u32[]{:S(2)}, u32[]{:S(2)}) collective-permute-start(f32[1,4352]{1,0:T(1,128)S(1)} %collective-permute-done.3.refs_7_), channel_id=1, source_target_pairs={{0,1},{1,0},{2,3},{3,2},{4,5},{5,4},{6,7},{7,6},{8,9},{9,8},{10,11... | collective-permute-start | bytes 52232 | tf_op jit(solution)/shard_map/ppermute | solution.py:334
  47.7 0.8 %collective-permute-done.4.refs_8_ = f32[1,4352]{1,0:T(1,128)S(1)} collective-permute-done((f32[1,4352]{1,0:T(1,128)S(1)}, f32[1,4352]{1,0:T(1,128)S(1)}, u32[]{:S(2)}, u32[]{:S(2)}) %collective-permute-start.4) | collective-permute-done | bytes 17440 | tf_op jit(solution)/shard_map/ppermute | solution.py:334
  48.5 0.0 all-to-all-done.refs_9_
  48.5 0.0 copy-done.1
  48.5 18.0 %shard_map.80 = (f32[1,4096]{1,0:T(1,128)}, f32[768,3840]{1,0:T(8,128)}) custom-call(s32[8,128]{1,0:T(8,128)S(1)} %bitcast.7, f32[768,128]{1,0:T(8,128)} %bitcast.10, f32[768,128]{1,0:T(8,128)} %bitcast.13, f32[768,128]{1,0:T(8,128)} %bitcast.16, f32[768,128]{1,0:T(8,128)} %bitcast.19, ...), custom_call_target="tpu_custom_call", output_to_operand_aliasing={{1}: (10, {})} | custom-call | tf_op jit(solution)/shard_map/pallas_call | solution.py:394
Async XLA Ops:
  0.6 0.7 %copy-start = (s32[128,8]{0,1:T(8,128)S(1)}, s32[128,8]{0,1:T(8,128)}, u32[]{:S(2)}) copy-start(s32[128,8]{0,1:T(8,128)} %param.11) | copy-start | bytes 12292
  13.4 16.7 %collective-permute-start.1 = (f32[1,4096]{1,0:T(1,128)S(1)}, f32[1,4096]{1,0:T(1,128)S(1)}, u32[]{:S(2)}, u32[]{:S(2)}) collective-permute-start(f32[1,4096]{1,0:T(1,128)S(1)} %get-tuple-element.14), channel_id=1, source_target_pairs={{0,127},{1,2},{2,1},{3,4},{4,3},{5,6},{6,5},{7,8},{8,7},{9,10},{10... | collective-permute-start | bytes 49160 | tf_op jit(solution)/shard_map/ppermute | solution.py:337
  17.9 30.6 %copy-start.1 = (s32[128,8]{0,1:T(8,128)S(1)}, s32[128,8]{0,1:T(8,128)}, u32[]{:S(2)}) copy-start(s32[128,8]{0,1:T(8,128)} %param.11) | copy-start | bytes 12292
  24.8 6.4 %collective-permute-start = (f32[1,8192]{1,0:T(1,128)S(1)}, f32[1,8192]{1,0:T(1,128)S(1)}, u32[]{:S(2)}, u32[]{:S(2)}) collective-permute-start(f32[1,8192]{1,0:T(1,128)S(1)} %get-tuple-element.13.pack_ref), channel_id=1, source_target_pairs={{0,1},{1,0},{2,3},{3,2},{4,5},{5,4},{6,7},{7,6},{8,9},{9,8},{10,11... | collective-permute-start | bytes 98312 | tf_op jit(solution)/shard_map/ppermute | solution.py:334
  30.0 1.2 %collective-permute-start.2 = (f32[1,4096]{1,0:T(1,128)S(1)}, f32[1,4096]{1,0:T(1,128)S(1)}, u32[]{:S(2)}, u32[]{:S(2)}) collective-permute-start(f32[1,4096]{1,0:T(1,128)S(1)} %collective-permute-done.1.far_ref), channel_id=1, source_target_pairs={{0,1},{1,0},{2,3},{3,2},{4,5},{5,4},{6,7},{7,6},{8,9},{9,8},{10,11... | collective-permute-start | bytes 49160 | tf_op jit(solution)/shard_map/ppermute | solution.py:334
  31.9 16.6 %all-to-all-start = ((f32[128,1,128]{2,1,0:T(1,128)}), f32[128,1,128]{2,1,0:T(1,128)S(1)}, u32[]{:S(2)}, u32[]{:S(2)}) async-start(f32[128,1,128]{2,1,0:T(1,128)} %get-tuple-element.18), calls=%async_computation | async-start | bytes 131072 | tf_op jit(solution)/shard_map/all_to_all | solution.py:392
  37.7 3.5 %collective-permute-start.3 = (f32[1,4352]{1,0:T(1,128)S(1)}, f32[1,4352]{1,0:T(1,128)S(1)}, u32[]{:S(2)}, u32[]{:S(2)}) collective-permute-start(f32[1,4352]{1,0:T(1,128)S(1)} %get-tuple-element.16.refs_5_), channel_id=1, source_target_pairs={{0,127},{1,2},{2,1},{3,4},{4,3},{5,6},{6,5},{7,8},{8,7},{9,10},{10... | collective-permute-start | bytes 52232 | tf_op jit(solution)/shard_map/ppermute | solution.py:337
  41.3 7.3 %collective-permute-start.4 = (f32[1,4352]{1,0:T(1,128)S(1)}, f32[1,4352]{1,0:T(1,128)S(1)}, u32[]{:S(2)}, u32[]{:S(2)}) collective-permute-start(f32[1,4352]{1,0:T(1,128)S(1)} %collective-permute-done.3.refs_7_), channel_id=1, source_target_pairs={{0,1},{1,0},{2,3},{3,2},{4,5},{5,4},{6,7},{7,6},{8,9},{9,8},{10,11... | collective-permute-start | bytes 52232 | tf_op jit(solution)/shard_map/ppermute | solution.py:334
